TPU v7x, 128 devices: a whole 4x4x4 slice. The times are simulated.
128 devices in a mesh: leaf: 4 (over y), row: 32 (over x, z, core).
Axes of the slice: x: 4, y: 4, z: 4, core: 2. Of those that a mesh axis runs over, the one named last changes fastest.
Arguments:
- rhs_sub: float32 [4, 2, 1024, 512], P('leaf', None, 'row'), may hold values from -6 to 6
- rhs_anc: float32 [16384, 512], P('row'), may hold values from -6 to 6
- inv_sub: float32 [4, 2, 1024, 1024], P('leaf', None, 'row'), may hold values from -3 to 3, as said below
- panel_mid: float32 [4, 1024, 1024], P('leaf', 'row'), may hold values from -0.1875 to 0.1875
- panel_anc: float32 [4, 2, 16384, 1024], P('leaf', None, 'row'), may hold values from -0.125 to 0.125
- block_mask: int32 [4, 2, 128], P('leaf', None, 'row'), may hold values 0 or 1
- inv_anc: float32 [16384, 1024], P('row'), may hold values from -3 to 3, as said below
Outputs:
- x_sub: float32 [4, 2, 1024, 512], P('leaf', None, 'row')
- x_anc: float32 [16384, 512], P('row')
Inputs may be any that keep to these rules, and one draw needn't show every extreme that they name: `inv_sub`: each [1024, 1024] block is lower triangular with its diagonal between 0.3 and 3. `inv_anc`: each block of 1024 rows has its diagonal between 0.3 and 3.
All inputs are finite; a program needn't handle non-finite values. No bound on the sum of `block_mask` on one device may be relied on, other than what follows from the above.
Results may differ from a plain program's by a relative error of at most 0.00012.
Values sent between devices are 32-bit elements; how exact they have to be, the bound alone decides.
A program may use at most 64 MiB of HBM per device.

v0:
```python
import jax
import jax.numpy as jnp
from jax import lax
from jax.sharding import PartitionSpec as P


def from_partner(value, axis, bit):
    mask = 2**bit
    pairs = [(source, source ^ mask) for source in range(lax.axis_size(axis))]
    return lax.ppermute(value, axis, pairs)


def product(left, right):
    return jnp.dot(left, right, precision=lax.Precision.HIGHEST, preferred_element_type=jnp.float32)


def transposed(left, right):
    return lax.dot_general(
        left,
        right,
        (((0,), (0,)), ((), ())),
        precision=lax.Precision.HIGHEST,
        preferred_element_type=jnp.float32,
    )


def solve_rows(matrix, rhs_local):
    return product(matrix, lax.all_gather(rhs_local, "row", axis=0, tiled=True))


def apply_rows(matrices, solution_local):
    piece = lax.all_gather(solution_local, "row", axis=0, tiled=True)
    return tuple((product(matrix, piece) for matrix in matrices))


def ancestor_solve(inverse_rows, values):
    rows_local = inverse_rows.shape[0]
    width = inverse_rows.shape[1]
    row_index = lax.axis_index("row")
    levels = (width // rows_local).bit_length() - 1
    whole = values
    bit_number = 0
    other = from_partner(whole, "row", bit_number)
    upper = row_index >> bit_number & 1
    whole = jnp.where(
        upper == 1, jnp.concatenate([other, whole], 0), jnp.concatenate([whole, other], 0)
    )
    forward = product(inverse_rows, whole)
    partial_value = transposed(inverse_rows, forward)
    for bit_number in reversed(range(levels)):
        half = partial_value.shape[0] // 2
        upper = row_index >> bit_number & 1
        keep = jnp.where(upper == 1, partial_value[half:], partial_value[:half])
        outgoing = jnp.where(upper == 1, partial_value[:half], partial_value[half:])
        partial_value = keep + from_partner(outgoing, "row", bit_number)
    return partial_value


def back_solve(matrix, values):
    return lax.psum_scatter(transposed(matrix, values), "row", scatter_dimension=0, tiled=True)


def per_device(rhs_sub, rhs_anc, inv_sub, panel_mid, panel_anc, block_mask, inv_anc):
    rhs_local = rhs_sub[0]
    inverses = inv_sub[0]
    middle = panel_mid[0]
    rows_local = panel_anc.shape[2]
    block_count = block_mask.shape[2]
    mask_rows = block_mask[0].astype(jnp.float32)
    panels = (
        panel_anc[0].reshape(2, block_count, rows_local // block_count, -1)
        * mask_rows[:, :, None, None]
    ).reshape(2, rows_local, -1)
    first = solve_rows(inverses[0], rhs_local[0])
    middle_first, update_first = apply_rows((middle, panels[0]), first)
    second = solve_rows(inverses[1], rhs_local[1] - middle_first)
    (update_second,) = apply_rows((panels[1],), second)
    partial_value = update_first + update_second
    total = lax.psum(partial_value, "leaf")
    x_anc = ancestor_solve(inv_anc, rhs_anc - total)
    second_sum = lax.psum_scatter(
        transposed(panels[1], x_anc), "row", scatter_dimension=0, tiled=True
    )
    x_second = back_solve(inverses[1], second - second_sum)
    ancestor_part = transposed(panels[0], x_anc)
    first_sum = lax.psum_scatter(
        ancestor_part + transposed(middle, x_second), "row", scatter_dimension=0, tiled=True
    )
    x_first = back_solve(inverses[0], first - first_sum)
    return (jnp.stack([x_first, x_second])[None], x_anc)


def solution(mesh):
    return jax.shard_map(
        per_device,
        mesh=mesh,
        in_specs=(
            P("leaf", None, "row", None),
            P("row", None),
            P("leaf", None, "row", None),
            P("leaf", "row", None),
            P("leaf", None, "row", None),
            P("leaf", None, "row"),
            P("row", None),
        ),
        out_specs=(P("leaf", None, "row", None), P("row", None)),
        check_vma=False,
    )
```

profile of v0, /device:TPU:1, one launch (start us, length us, event | category | flops | bytes accessed | tf_op | source)
XLA Modules:
  0.0 626.5 jit_solution(943038408354954291)
XLA Ops:
  7.2 1.6 slice.37
  9.0 49.5 %all-gather.12.cloned.1.call-done = f32[1,1,1024,512]{3,2,1,0:T(8,128)} async-done(((f32[1,1,32,512]{3,2,1,0:T(8,128)}), f32[1,1,1024,512]{3,2,1,0:T(8,128)}) %all-gather.12.cloned.1.call-update) | async-done | bytes 2097168 | tf_op jit(solution)/shard_map/all_gather | solution.py:28
  58.5 3.6 fusion.6
  62.2 43.3 %all-gather.6.cloned.1.call-done = f32[1024,512]{1,0:T(8,128)} async-done(((f32[32,512]{1,0:T(8,128)}), f32[1024,512]{1,0:T(8,128)}) %all-gather.6.cloned.1.call-update) | async-done | bytes 2097168 | tf_op jit(solution)/shard_map/all_gather | solution.py:32
  105.5 3.6 fusion.8
  109.1 43.3 %all-gather.8.cloned.1.call-done = f32[1024,512]{1,0:T(8,128)} async-done(((f32[32,512]{1,0:T(8,128)}), f32[1024,512]{1,0:T(8,128)}) %all-gather.8.cloned.1.call-update) | async-done | bytes 2097168 | tf_op jit(solution)/shard_map/all_gather | solution.py:28
  152.5 3.6 convolution_bitcast_fusion.3
  156.1 2.7 broadcast_multiply_fusion
  158.8 1.8 fusion.24
  160.6 1.3 copy-done.1
  161.9 3.5 fusion.25
  165.5 34.0 %all-gather.10.cloned.1.call-done = f32[1024,512]{1,0:T(8,128)} async-done(((f32[32,512]{1,0:T(8,128)}), f32[1024,512]{1,0:T(8,128)}) %all-gather.10.cloned.1.call-update) | async-done | bytes 2097168 | tf_op jit(solution)/shard_map/all_gather | solution.py:32
  199.4 6.7 %convolution_add_fusion = f32[512,512]{1,0:T(8,128)} fusion(f32[512,512]{1,0:T(8,128)S(1)} %fusion.25, f32[512,1024]{1,0:T(8,128)} %bitcast.61, f32[1024,512]{1,0:T(8,128)} %all-gather.10.cloned.1.call-done), kind=kOutput, calls=%fused_computation.14 | convolution fusion | flops 3221487616 | bytes 6291456 | tf_op jit(solution)/shard_map/dot_general | solution.py:14
  206.2 43.3 %all-reduce.2.cloned.1.call-done = f32[512,512]{1,0:T(8,128)} async-done(((f32[512,512]{1,0:T(8,128)}), f32[512,512]{1,0:T(8,128)}) %all-reduce.2.cloned.1.call-update) | async-done | bytes 1048592 | tf_op jit(solution)/shard_map/psum | solution.py:79
  249.5 1.7 sub.13
  251.2 2.3 collective-permute-start
  253.6 2.4 collective-permute-done
  256.0 8.3 %fusion = f32[512,512]{1,0:T(8,128)S(1)} fusion(f32[512,1024]{1,0:T(8,128)S(1)} %copy-done, f32[512,512]{1,0:T(8,128)S(1)} %sub.13, f32[512,512]{1,0:T(8,128)} %collective-permute-done, pred[]{:T(512)S(6)} %eq.2), kind=kOutput, calls=%fused_computation.1 | convolution fusion | flops 3222798336 | bytes 5242881 | tf_op jit(solution)/shard_map/dot_general | solution.py:14
  264.3 3.6 convolution_bitcast_fusion.2
  268.8 2.3 collective-permute-done.1
  271.4 8.2 %fusion.26 = f32[1024,512]{1,0:T(8,128)} fusion(f32[512,1024]{1,0:T(8,128)S(1)} %bitcast.62, f32[512,512]{0,1:T(8,128)S(1)} %select_add_fusion), kind=kOutput, calls=%fused_computation.39 | convolution fusion | flops 3221225472 | bytes 5242880 | tf_op jit(solution)/shard_map/dot_general | solution.py:18
  279.7 78.0 %reduce-scatter.9.cloned.1.call-done = f32[32,512]{1,0:T(8,128)} async-done(((f32[1024,512]{1,0:T(8,128)}), f32[32,512]{1,0:T(8,128)}) %reduce-scatter.9.cloned.1.call-update) | async-done | bytes 65552 | tf_op jit(solution)/shard_map/reduce_scatter | solution.py:81
  357.7 4.0 convolution_bitcast_fusion.1
  361.7 2.9 copy.14
  364.9 78.1 %reduce-scatter.13.cloned.1.call-done = f32[32,512]{1,0:T(8,128)} async-done(((f32[1024,512]{1,0:T(8,128)}), f32[32,512]{1,0:T(8,128)}) %reduce-scatter.13.cloned.1.call-update) | async-done | bytes 65552
  443.0 2.8 fusion.12
  445.9 8.2 %bitcast_add_fusion = f32[1024,512]{1,0:T(8,128)} fusion(f32[512,1024]{0,1:T(8,128)S(1)} %fusion.12, f32[512,1024]{1,0:T(8,128)S(1)} %bitcast.60, f32[512,512]{0,1:T(8,128)S(1)} %select_add_fusion), kind=kOutput, calls=%fused_computation.7 | convolution fusion | flops 3221749760 | bytes 7340032 | tf_op jit(solution)/shard_map/dot_general | solution.py:18
  454.2 78.3 %reduce-scatter.11.cloned.1.call-done = f32[32,512]{1,0:T(8,128)} async-done(((f32[1024,512]{1,0:T(8,128)}), f32[32,512]{1,0:T(8,128)}) %reduce-scatter.11.cloned.1.call-update) | async-done | bytes 65552 | tf_op jit(solution)/shard_map/reduce_scatter | solution.py:86
  532.5 4.0 convolution_bitcast_fusion
  536.5 2.9 copy.16
  539.4 1.3 copy.13
  540.9 76.8 %reduce-scatter.15.cloned.1.call-done = f32[32,512]{1,0:T(8,128)} async-done(((f32[1024,512]{1,0:T(8,128)}), f32[32,512]{1,0:T(8,128)}) %reduce-scatter.15.cloned.1.call-update) | async-done | bytes 65552
  (52 shorter events, 4.0 us)
Async XLA Ops:
  7.2 248.8 %copy-start = (f32[512,1024]{1,0:T(8,128)S(1)}, f32[512,1024]{1,0:T(8,128)}, u32[]{:S(2)}) copy-start(f32[512,1024]{1,0:T(8,128)} %param.13) | copy-start | bytes 6291460
  7.2 98.3 %copy-start.11 = (f32[1,2,32,512]{3,2,1,0:T(8,128)S(1)}, f32[1,2,32,512]{3,2,1,0:T(8,128)}, u32[]{:S(2)}) copy-start(f32[1,2,32,512]{3,2,1,0:T(8,128)} %param.7) | copy-start | bytes 393220
  7.2 98.3 %copy-start.8 = (f32[1,32,1024]{2,1,0:T(8,128)S(1)}, f32[1,32,1024]{2,1,0:T(8,128)}, u32[]{:S(2)}) copy-start(f32[1,32,1024]{2,1,0:T(8,128)} %param.10) | copy-start | bytes 393220
  7.2 51.3 %all-gather.12.cloned.1.call-start = ((), (), s32[]{:S(2)}) async-start(), calls=%async_computation.10 | async-start | bytes 2162688 | tf_op jit(solution)/shard_map/all_gather | solution.py:28
  8.9 143.6 %copy-start.5 = (f32[1,2,32,1024]{3,2,1,0:T(8,128)S(1)}, f32[1,2,32,1024]{3,2,1,0:T(8,128)}, u32[]{:S(2)}) copy-start(f32[1,2,32,1024]{3,2,1,0:T(8,128)} %param.9) | copy-start | bytes 786436
  8.9 96.6 %all-gather.6.cloned.1.call-start = ((), (), s32[]{:S(2)}) async-start(), calls=%async_computation.4 | async-start | bytes 2162688 | tf_op jit(solution)/shard_map/all_gather | solution.py:32
  62.1 94.0 %copy-start.12 = (s32[1,2,4]{2,1,0:T(2,128)S(1)}, s32[1,2,4]{2,1,0:T(2,128)}, u32[]{:S(2)}) copy-start(s32[1,2,4]{2,1,0:T(2,128)} %param.12) | copy-start | bytes 100
  62.1 90.3 %all-gather.8.cloned.1.call-start = ((), (), s32[]{:S(2)}) async-start(), calls=%async_computation.5 | async-start | bytes 2162688 | tf_op jit(solution)/shard_map/all_gather | solution.py:28
  109.1 90.3 %all-gather.10.cloned.1.call-start = ((), (), s32[]{:S(2)}) async-start(), calls=%async_computation.6 | async-start | bytes 2162688 | tf_op jit(solution)/shard_map/all_gather | solution.py:32
  156.1 93.4 %all-reduce.2.cloned.1.call-start = ((), (), s32[]{:S(2)}) async-start(), calls=%async_computation.7 | async-start | bytes 2097152 | tf_op jit(solution)/shard_map/psum | solution.py:79
  158.8 3.1 copy-start.4
  160.6 1.3 copy-start.1
  206.2 151.5 %reduce-scatter.9.cloned.1.call-start = ((), (), s32[]{:S(2)}) async-start(), calls=%async_computation.8 | async-start | bytes 2162688 | tf_op jit(solution)/shard_map/reduce_scatter | solution.py:81
  251.2 4.8 collective-permute-start
  268.1 3.3 copy-start.3
  268.1 3.0 collective-permute-start.1
  279.6 78.1 %copy-start.7 = (f32[32,512]{1,0:T(8,128)S(1)}, f32[32,512]{1,0:T(8,128)}, u32[]{:S(2)}) copy-start(f32[32,512]{1,0:T(8,128)} %convolution_bitcast_fusion.3) | copy-start | bytes 196612
  279.6 163.4 %reduce-scatter.13.cloned.1.call-start = ((), (), s32[]{:S(2)}) async-start(), calls=%async_computation.11 | async-start | bytes 2162688
  364.6 78.4 %copy-start.9 = (f32[1,32,1024]{2,1,0:T(8,128)S(1)}, f32[1,32,1024]{2,1,0:T(8,128)}, u32[]{:S(2)}) copy-start(f32[1,32,1024]{2,1,0:T(8,128)} %param.10) | copy-start | bytes 393220
  364.6 167.8 %reduce-scatter.11.cloned.1.call-start = ((), (), s32[]{:S(2)}) async-start(), calls=%async_computation.9 | async-start | bytes 2162688 | tf_op jit(solution)/shard_map/reduce_scatter | solution.py:86
  443.0 2.8 copy-start.2
  454.1 78.4 %copy-start.6 = (f32[32,512]{1,0:T(8,128)S(1)}, f32[32,512]{1,0:T(8,128)}, u32[]{:S(2)}) copy-start(f32[32,512]{1,0:T(8,128)} %fusion.6) | copy-start | bytes 196612
  454.1 163.6 %reduce-scatter.15.cloned.1.call-start = ((), (), s32[]{:S(2)}) async-start(), calls=%async_computation.12 | async-start | bytes 2162688
  539.4 1.3 copy-start.10
Sparse Core Ops, SparseCore 0:
  10.9 47.5 all-gather.11
  62.2 43.2 all-gather.5
  109.2 43.2 all-gather.7
  156.2 43.2 all-gather.9
  206.3 43.1 all-reduce.1
  279.7 77.9 reduce-scatter.8
  364.8 78.2 reduce-scatter.12
  454.2 78.1 reduce-scatter.10
  539.5 78.1 reduce-scatter.14
where the time goes:
time: 636 us; the launch traced here: 626 us
  waiting for transfers between devices  530 us (83%)
  matrix products  60 us (9%)
  between operations  14.5 us (2%)
  local copies, waits for them, and re-layouts  13.2 us (2%)
    unnamed x11, waiting for transfers between devices  155 us
    all_gather x2, waiting for transfers between devices, solve_rows(): return product(matrix, lax.all_gather(rhs_local, 'row', axis=0, tiled=True))  92.9 us
    reduce_scatter x1, waiting for transfers between devices, per_device(): lax.psum_scatter(ancestor_part + transposed(middle, x_second), 'row', sca...  78.3 us
    reduce_scatter x1, waiting for transfers between devices, per_device(): lax.psum_scatter(transposed(panels[1], x_anc), 'row', scatter_dimension=0...  78 us
    all_gather x2, waiting for transfers between devices, apply_rows(): piece = lax.all_gather(solution_local, 'row', axis=0, tiled=True)  77.3 us
    psum x1, waiting for transfers between devices, per_device(): total = lax.psum(partial_value, 'leaf')  43.3 us
    dot_general x6, matrix products, transposed(): lax.dot_general(left, right, (((0,), (0,)), ((), ())), precision=lax.Prec...  30.8 us
    dot_general x6, matrix products, product(): jnp.dot(left, right, precision=lax.Precision.HIGHEST, preferred_element_t...  29.2 us
  transfers between devices with their start and end apart: 11, of which 11 were waited for; matrix products, arithmetic and copies ran while one was open for 2% of the time, Pallas kernels for 0%

commit v1 on v0

v1 whole, which is shorter than its diff:
```python
import functools

import jax
import jax.numpy as jnp
from jax import lax
from jax.experimental import pallas as pl
from jax.experimental.pallas import tpu as pltpu
from jax.sharding import PartitionSpec as P

F32 = jnp.float32
BF16 = jnp.bfloat16
MESH = pl.DeviceIdType.MESH
COPIES = 192


def split(value):
    high = value.astype(BF16)
    return high, (value - high.astype(F32)).astype(BF16)


def dot(left, right):
    return jnp.dot(left, right, preferred_element_type=F32)


def product(left, right):
    left_high, left_low = left
    right_high, right_low = right
    return dot(left_high, right_high) + (dot(left_high, right_low) + dot(left_low, right_high))


def kernel(
    rhs_sub, rhs_anc, inv_sub, panel_mid, panel_anc, mask, inv_anc,
    x_sub, x_anc,
    rhs0, rhs1, inv0, inv1, mid, panels, anc, anc_rhs,
    tee, first, second, op_high, op_low, first_high, first_low,
    update, y_in, value, fwd_t, x_t, x_out, z_t, w_t,
    w_send, r_first, r_sum, r_second, out_sub, mask_tile,
    send_sem, recv_sem, local_sem,
):
    y = lax.axis_index("leaf")
    r = lax.axis_index("row")
    x, z, c = r // 8, (r // 2) % 4, r % 2
    o = 1 - c

    def at_x(d):
        return (y, ((x + d) % 4) * 8 + z * 2 + c)

    def at_z(d):
        return (y, x * 8 + ((z + d) % 4) * 2 + c)

    def at_y(d):
        return ((y + d) % 4, r)

    sibling = (y, x * 8 + z * 2 + o)

    count = [0, 0]
    sends = []

    def remote(src, dst, landing, device):
        index = count[0]
        count[0] += 1
        out = pltpu.make_async_remote_copy(
            src_ref=src, dst_ref=dst, send_sem=send_sem.at[index], recv_sem=recv_sem.at[index],
            device_id=device, device_id_type=MESH,
        )
        out.start()
        sends.append(out)
        into = pltpu.make_async_remote_copy(
            src_ref=landing, dst_ref=landing, send_sem=send_sem.at[index], recv_sem=recv_sem.at[index],
            device_id=device, device_id_type=MESH,
        )
        return into.wait_recv

    def local(src, dst):
        index = count[1]
        count[1] += 1
        copy = pltpu.make_async_copy(src, dst, local_sem.at[index])
        copy.start()
        return copy.wait

    def wait_all(waits):
        for wait in waits:
            wait()

    def columns(core, half):
        return pl.ds(pl.multiple_of(core * 256 + half * 128, 128), 128)

    mine = pl.ds(pl.multiple_of(c * 32, 32), 32)
    theirs = pl.ds(pl.multiple_of(o * 32, 32), 32)

    load_rhs = []
    for h in range(2):
        load_rhs.append(local(rhs_sub.at[0, 0, :, columns(c, h)], rhs0.at[h, x, z, mine]))
    load_inv0 = [local(inv_sub.at[0, 0, pl.ds(16 * h, 16)], inv0.at[x, z, c, h]) for h in range(2)]
    load_mid = [local(panel_mid.at[0, pl.ds(16 * h, 16)], mid.at[x, z, c, h]) for h in range(2)]
    load_rhs1 = [local(rhs_sub.at[0, 1, :, columns(c, h)], rhs1.at[h, mine]) for h in range(2)]
    load_inv1 = [local(inv_sub.at[0, 1, pl.ds(16 * h, 16)], inv1.at[x, z, c, h]) for h in range(2)]
    load_panels = [local(panel_anc.at[0, s], panels.at[s, c]) for s in range(2)]
    both = pl.ds(pl.multiple_of(c * 256, 256), 256)
    other = pl.ds(pl.multiple_of(o * 256, 256), 256)
    load_anc = [local(inv_anc, anc.at[c]), local(rhs_anc.at[:, both], anc_rhs.at[c])]
    for s in range(2):
        for j in range(4):
            mask_tile[c, s, j] = jnp.full((8, 128), mask[0, s, j].astype(F32), F32)

    barrier = pltpu.get_barrier_semaphore()
    for device in [at_x(1), at_x(2), at_x(3), at_z(1), at_z(2), at_z(3), at_y(1), at_y(2), at_y(3), sibling]:
        pl.semaphore_signal(barrier, inc=1, device_id=device, device_id_type=MESH)
    pl.semaphore_wait(barrier, 10)

    swap_rhs0 = [
        remote(rhs_sub.at[0, 0, :, columns(o, h)], rhs0.at[h, x, z, mine], rhs0.at[h, x, z, theirs], sibling)
        for h in range(2)
    ]
    swap_rhs1 = [
        remote(rhs_sub.at[0, 1, :, columns(o, h)], rhs1.at[h, mine], rhs1.at[h, theirs], sibling)
        for h in range(2)
    ]
    swap_mask = [remote(mask_tile.at[c], mask_tile.at[c], mask_tile.at[o], sibling)]

    def vector_one(ref):
        along_z = [remote(ref.at[0, x, z], ref.at[0, x, z], ref.at[0, x, (z - d) % 4], at_z(d)) for d in (1, 3, 2)]
        along_x = [remote(ref.at[1, x, z], ref.at[1, x, z], ref.at[1, (x - d) % 4, z], at_x(d)) for d in (1, 3, 2)]
        return along_z, along_x

    def vector_two(ref, waits):
        along_z, along_x = waits
        wait_all(along_z)
        then_x = [remote(ref.at[0, x], ref.at[0, x], ref.at[0, (x - d) % 4], at_x(d)) for d in (1, 3, 2)]
        wait_all(along_x)
        then_z = [
            remote(ref.at[1, :, z], ref.at[1, :, z], ref.at[1, :, (z - d) % 4], at_z(d)) for d in (1, 3, 2)
        ]
        return then_x + then_z

    def matrix_one(ref):
        along_z = [
            remote(ref.at[x, z, c, 0], ref.at[x, z, c, 0], ref.at[x, (z - d) % 4, c, 0], at_z(d)) for d in (1, 3, 2)
        ]
        along_x = [
            remote(ref.at[x, z, c, 1], ref.at[x, z, c, 1], ref.at[(x - d) % 4, z, c, 1], at_x(d)) for d in (1, 3, 2)
        ]
        return along_z, along_x

    def matrix_pass(ref):
        return [remote(ref.at[x, z, c], ref.at[x, z, c], ref.at[x, z, o], sibling)]

    def matrix_two(ref, waits):
        along_z, along_x = waits
        passed = []
        wait_all(along_z)
        then_x = [
            remote(ref.at[x, :, c, 0], ref.at[x, :, c, 0], ref.at[(x - d) % 4, :, c, 0], at_x(d)) for d in (1, 3, 2)
        ]
        wait_all(along_x)
        then_z = [
            remote(ref.at[:, z, c, 1], ref.at[:, z, c, 1], ref.at[:, (z - d) % 4, c, 1], at_z(d)) for d in (1, 3, 2)
        ]
        for d in (1, 3, 2):
            k = (z - d) % 4
            passed.append(remote(ref.at[x, k, c, 0], ref.at[x, k, c, 0], ref.at[x, k, o, 0], sibling))
            k = (x - d) % 4
            passed.append(remote(ref.at[k, z, c, 1], ref.at[k, z, c, 1], ref.at[k, z, o, 1], sibling))
        return then_x, then_z, passed

    def matrix_end(ref, waits):
        then_x, then_z, passed = waits
        for n, d in enumerate((1, 3, 2)):
            k = (x - d) % 4
            then_x[n]()
            passed.append(remote(ref.at[k, :, c, 0], ref.at[k, :, c, 0], ref.at[k, :, o, 0], sibling))
            k = (z - d) % 4
            then_z[n]()
            passed.append(remote(ref.at[:, k, c, 1], ref.at[:, k, c, 1], ref.at[:, k, o, 1], sibling))
        return passed

    def hold(ref):
        for h in range(2):
            high, low = split(ref[h].reshape(1024, 128))
            op_high[:, 128 * h:128 * h + 128] = high
            op_low[:, 128 * h:128 * h + 128] = low

    wait_all(load_rhs)
    wait_all(swap_rhs0)
    rhs0_one = vector_one(rhs0)
    wait_all(load_inv0)
    inv0_pass = matrix_pass(inv0)
    inv0_one = matrix_one(inv0)
    rhs0_two = vector_two(rhs0, rhs0_one)
    inv0_two = matrix_two(inv0, inv0_one)
    wait_all(load_mid)
    mid_pass = matrix_pass(mid)
    wait_all(load_inv1)
    inv1_pass = matrix_pass(inv1)
    inv1_one = matrix_one(inv1)
    swap_panel0 = [remote(panel_anc.at[0, 0], panels.at[0, c], panels.at[0, o], sibling)]
    wait_all(swap_mask)
    wait_all(rhs0_two)
    hold(rhs0)
    inv0_end = matrix_end(inv0, inv0_two)
    inv1_two = matrix_two(inv1, inv1_one)
    wait_all(inv0_pass)
    wait_all(inv0_end)

    @pl.loop(0, 4)
    def _(i):
        got = product(split(inv0[i].reshape(256, 1024)), (op_high[...], op_low[...]))
        rows = pl.ds(pl.multiple_of(i * 256, 256), 256)
        first[rows] = got
        high, low = split(got)
        first_high[rows] = high
        first_low[rows] = low

    wait_all(load_rhs1)
    wait_all(swap_rhs1)
    wait_all(mid_pass)
    got = product(split(mid[x, z].reshape(64, 1024)), (first_high[...], first_low[...]))
    for h in range(2):
        tee[h, x, z] = rhs1[h] - got[:, 128 * h:128 * h + 128]
    tee_one = vector_one(tee)
    tee_two = vector_two(tee, tee_one)
    swap_panel1 = [remote(panel_anc.at[0, 1], panels.at[1, c], panels.at[1, o], sibling)]

    def masked(s):
        for core in range(2):
            for j in range(4):
                scale = mask_tile[core, s, j][0:1, 0:1]
                panels[s, core, 128 * j:128 * j + 128] = panels[s, core, 128 * j:128 * j + 128] * scale

    wait_all(load_panels)
    wait_all(swap_panel0)
    masked(0)

    @pl.loop(0, 4)
    def _(i):
        block = panels[0, i // 2, pl.ds(pl.multiple_of((i % 2) * 256, 256), 256)]
        update[i] = product(split(block), (first_high[...], first_low[...]))

    inv1_end = matrix_end(inv1, inv1_two)
    mid_one = matrix_one(mid)
    wait_all(swap_panel1)
    masked(1)
    wait_all(tee_two)
    hold(tee)
    wait_all(inv1_pass)
    wait_all(inv1_end)

    @pl.loop(0, 4)
    def _(i):
        got = product(split(inv1[i].reshape(256, 1024)), (op_high[...], op_low[...]))
        rows = pl.ds(pl.multiple_of(i * 256, 256), 256)
        second[rows] = got

    high, low = split(second[...])
    op_high[...] = high
    op_low[...] = low

    def update_block(i):
        block = panels[1, i // 2, pl.ds(pl.multiple_of((i % 2) * 256, 256), 256)]
        update[i] = update[i] + product(split(block), (op_high[...], op_low[...]))

    update_in = []
    for d in (1, 3, 2):
        k = (y + d) % 4
        update_block(k)
        update_in.append(remote(update.at[k], y_in.at[d - 1], y_in.at[d - 1], at_y(d)))
    update_block(y)
    mid_two = matrix_two(mid, mid_one)

    swap_anc = [
        remote(rhs_anc.at[:, other], anc_rhs.at[c], anc_rhs.at[o], sibling),
        remote(inv_anc, anc.at[c], anc.at[o], sibling),
    ]

    piece = x * 4 + z
    row = lax.broadcasted_iota(jnp.int32, (1024, 256), 0)
    inside = (row >= piece * 64) & (row < piece * 64 + 64)
    for s, solved in enumerate((first, second)):
        z_t[s] = jnp.where(inside, solved[...], 0.0).T

    wait_all(load_anc)
    wait_all(swap_anc[:1])
    wait_all(update_in)
    rows = pl.ds(pl.multiple_of((y % 2) * 256, 256), 256)
    value[y] = anc_rhs[y // 2, rows] - (update[y] + y_in[0] + y_in[1] + y_in[2])
    value_in = [remote(value.at[y], value.at[y], value.at[(y - d) % 4], at_y(d)) for d in (1, 3, 2)]
    mid_end = matrix_end(mid, mid_two)
    wait_all(swap_anc[1:])
    wait_all(mid_end)
    wait_all(value_in)
    high, low = split(value[...].reshape(1024, 256))
    op_high[...] = high
    op_low[...] = low

    @pl.loop(0, 4)
    def _(i):
        block = anc[i // 2, pl.ds(pl.multiple_of((i % 2) * 256, 256), 256)]
        got = product(split(block), (op_high[...], op_low[...]))
        fwd_t[:, pl.ds(pl.multiple_of(i * 256, 256), 256)] = got.T

    @pl.loop(0, 4)
    def _(n):
        cols = pl.ds(pl.multiple_of(n * 256, 256), 256)
        got = product(split(fwd_t[...]), split(anc[:, :, cols].reshape(1024, 256)))
        x_t[:, cols] = got
        x_out[n // 2, pl.ds(pl.multiple_of((n % 2) * 256, 256), 256)] = got.T

    done = [remote(x_out.at[o], x_anc.at[:, both], x_anc.at[:, other], sibling)]
    done.append(local(x_out.at[c], x_anc.at[:, both]))

    def reduce_one(s):
        along_x = [
            remote(w_send.at[s, 0, (x + d) % 4], r_first.at[s, 0, d - 1], r_first.at[s, 0, d - 1], at_x(d))
            for d in (1, 3, 2)
        ]
        along_z = [
            remote(w_send.at[s, 1, :, (z + d) % 4], r_first.at[s, 1, d - 1], r_first.at[s, 1, d - 1], at_z(d))
            for d in (1, 3, 2)
        ]
        return along_x, along_z

    def reduce_two(s, waits):
        along_x, along_z = waits
        wait_all(along_x)
        r_sum[s, 0] = (w_send[s, 0, x] + r_first[s, 0, 0]) + (r_first[s, 0, 1] + r_first[s, 0, 2])
        then_z = [
            remote(r_sum.at[s, 0, (z + d) % 4], r_second.at[s, 0, d - 1], r_second.at[s, 0, d - 1], at_z(d))
            for d in (1, 3, 2)
        ]
        wait_all(along_z)
        r_sum[s, 1] = (w_send[s, 1, :, z] + r_first[s, 1, 0]) + (r_first[s, 1, 1] + r_first[s, 1, 2])
        then_x = [
            remote(r_sum.at[s, 1, (x + d) % 4], r_second.at[s, 1, d - 1], r_second.at[s, 1, d - 1], at_x(d))
            for d in (1, 3, 2)
        ]
        return then_z + then_x

    def reduce_end(s, waits):
        wait_all(waits)
        for h, place in enumerate((z, x)):
            total = (r_sum[s, h, place] + r_second[s, h, 0]) + (r_second[s, h, 1] + r_second[s, h, 2])
            out_sub[s, :, 128 * h:128 * h + 128] = total
        out = remote(out_sub.at[s, theirs], x_sub.at[0, s, :, both], x_sub.at[0, s, :, other], sibling)
        return [out, local(out_sub.at[s, mine], x_sub.at[0, s, :, both])]

    def back(s, ref):
        @pl.loop(0, 4)
        def _(n):
            cols = pl.ds(pl.multiple_of(n * 256, 256), 256)
            got = product(split(z_t[s]), split(ref[:, :, :, :, :, cols].reshape(1024, 256)))
            if s == 1:
                w_t[:, cols] = got
            for h in range(2):
                w_send[s, h, n] = got[128 * h:128 * h + 128].T.reshape(4, 64, 128)

    @pl.loop(0, 4)
    def _(n):
        cols = pl.ds(pl.multiple_of(n * 256, 256), 256)
        z_t[1, :, cols] -= product(split(x_t[...]), split(panels[1, :, :, cols].reshape(1024, 256)))

    back(1, inv1)
    second_one = reduce_one(1)

    @pl.loop(0, 4)
    def _(n):
        cols = pl.ds(pl.multiple_of(n * 256, 256), 256)
        total = product(split(x_t[...]), split(panels[0, :, :, cols].reshape(1024, 256)))
        total += product(split(w_t[...]), split(mid[:, :, :, :, :, cols].reshape(1024, 256)))
        z_t[0, :, cols] -= total

    back(0, inv0)
    first_one = reduce_one(0)
    second_two = reduce_two(1, second_one)
    first_two = reduce_two(0, first_one)
    done += reduce_end(1, second_two)
    done += reduce_end(0, first_two)
    wait_all(done)
    for copy in sends:
        copy.wait_send()


def per_device(rhs_sub, rhs_anc, inv_sub, panel_mid, panel_anc, block_mask, inv_anc):
    any_space = pl.BlockSpec(memory_space=pl.ANY)
    vmem = pltpu.VMEM
    return pl.pallas_call(
        kernel,
        out_shape=(
            jax.ShapeDtypeStruct((1, 2, 32, 512), F32),
            jax.ShapeDtypeStruct((512, 512), F32),
        ),
        in_specs=[any_space] * 5 + [pl.BlockSpec(memory_space=pltpu.SMEM), any_space],
        out_specs=(any_space, any_space),
        scratch_shapes=[
            vmem((2, 4, 4, 64, 128), F32),
            vmem((2, 64, 128), F32),
            vmem((4, 4, 2, 2, 16, 1024), F32),
            vmem((4, 4, 2, 2, 16, 1024), F32),
            vmem((4, 4, 2, 2, 16, 1024), F32),
            vmem((2, 2, 512, 1024), F32),
            vmem((2, 512, 1024), F32),
            vmem((2, 512, 256), F32),
            vmem((2, 4, 4, 64, 128), F32),
            vmem((1024, 256), F32),
            vmem((1024, 256), F32),
            vmem((1024, 256), BF16),
            vmem((1024, 256), BF16),
            vmem((1024, 256), BF16),
            vmem((1024, 256), BF16),
            vmem((4, 256, 256), F32),
            vmem((3, 256, 256), F32),
            vmem((4, 256, 256), F32),
            vmem((256, 1024), F32),
            vmem((256, 1024), F32),
            vmem((2, 512, 256), F32),
            vmem((2, 256, 1024), F32),
            vmem((256, 1024), F32),
            vmem((2, 2, 4, 4, 64, 128), F32),
            vmem((2, 2, 3, 4, 64, 128), F32),
            vmem((2, 2, 4, 64, 128), F32),
            vmem((2, 2, 3, 64, 128), F32),
            vmem((2, 64, 256), F32),
            vmem((2, 2, 4, 8, 128), F32),
            pltpu.SemaphoreType.DMA((COPIES,)),
            pltpu.SemaphoreType.DMA((COPIES,)),
            pltpu.SemaphoreType.DMA((32,)),
        ],
        compiler_params=pltpu.CompilerParams(
            collective_id=0, has_side_effects=True, vmem_limit_bytes=60 * 2**20
        ),
        cost_estimate=pl.CostEstimate(flops=3 * 2 * 2900 * 2**20, bytes_accessed=10 * 2**20, transcendentals=0),
        name="solve",
    )(rhs_sub, rhs_anc, inv_sub, panel_mid, panel_anc, block_mask, inv_anc)


def solution(mesh):
    return jax.shard_map(
        per_device,
        mesh=mesh,
        in_specs=(
            P("leaf", None, "row", None),
            P("row", None),
            P("leaf", None, "row", None),
            P("leaf", "row", None),
            P("leaf", None, "row", None),
            P("leaf", None, "row"),
            P("row", None),
        ),
        out_specs=(P("leaf", None, "row", None), P("row", None)),
        check_vma=False,
    )
```

time: 636 us -> 126 us (0.20); the launches traced: 626 us -> 126 us
  waiting for transfers between devices: 530 us -> 0 us
  Pallas kernels: 0 us -> 122 us
  matrix products: 60 us -> 0 us
  between operations: 14.5 us -> 0.64 us
  local copies, waits for them, and re-layouts: 13.2 us -> 3.83 us
    all_gather x4 -> x0, waiting for transfers between devices: 170 us -> none  [the longest x2 92.9 us: solve_rows(): return product(matrix, lax.all_gather(rhs_local, 'row', axis=0, tiled=True))]
    reduce_scatter x2 -> x0, waiting for transfers between devices: 156 us -> none  [the longest x1 78.3 us: per_device(): lax.psum_scatter(ancestor_part + transposed(middle, x_second), 'row', sca...]
    unnamed x11 -> x0, waiting for transfers between devices: 155 us -> none
    pallas_call x0 -> x1, Pallas kernels: none -> 122 us  [per_device(): pl.pallas_call(kernel, out_shape=(jax.ShapeDtypeStruct((1, 2, 32, 512), F...]
    dot_general x12 -> x0, matrix products: 60 us -> none  [the longest x6 30.8 us: transposed(): lax.dot_general(left, right, (((0,), (0,)), ((), ())), precision=lax.Prec...]
    psum x1 -> x0, waiting for transfers between devices: 43.3 us -> none  [per_device(): total = lax.psum(partial_value, 'leaf')]
  transfers between devices with their start and end apart: 11 -> 0, of which waited for: 11 -> 0; matrix products, arithmetic and copies ran while one was open for 2% -> 0% of each run, Pallas kernels for 0% -> 0%
where the time goes in v1:
time: 126 us
  Pallas kernels  122 us (97%)
  local copies, waits for them, and re-layouts  3.83 us (3%)
    pallas_call x1, Pallas kernels, per_device(): pl.pallas_call(kernel, out_shape=(jax.ShapeDtypeStruct((1, 2, 32, 512), F...  122 us
    unnamed x2, local copies, waits for them, and re-layouts  3.83 us

profile of v1, /device:TPU:1, one launch (start us, length us, event | category | flops | bytes accessed | tf_op | source)
XLA Modules:
  0.0 126.2 jit_solution(4531448424382480145)
XLA Ops:
  0.6 121.7 %solve.1 = (f32[1,2,32,512]{3,2,1,0:T(8,128)}, f32[512,512]{1,0:T(8,128)}) custom-call(f32[1,2,32,512]{3,2,1,0:T(8,128)} %rhs_sub.1, f32[512,512]{1,0:T(8,128)} %rhs_anc.1, f32[1,2,32,1024]{3,2,1,0:T(8,128)} %inv_sub.1, f32[1,32,1024]{2,1,0:T(8,128)} %panel_mid.1, f32[1,2,512,1024]{3,2,1,0:T(8,128)} %panel_anc.1, s32[1,2,4]{2,1,0:T(2,128)} %mask.1, ...), custom_call_target="tpu_custom_call" | custom-call | flops 18245222400 | bytes 10485760 | tf_op jit(solution)/shard_map/solve/pallas_call | solution.py:385
  122.4 1.6 %copy.11 = f32[1,2,32,512]{3,2,1,0:T(8,128)} copy(f32[1,2,32,512]{3,2,1,0:T(8,128)} %get-tuple-element.4) | data formatting | bytes 262144
  123.9 2.3 %copy.12 = f32[512,512]{1,0:T(8,128)} copy(f32[512,512]{1,0:T(8,128)} %get-tuple-element.5) | data formatting | bytes 2097152

commit v2 on v0

v2 whole, which is shorter than its diff:
```python
import functools

import jax
import jax.numpy as jnp
from jax import lax
from jax.experimental import pallas as pl
from jax.experimental.pallas import tpu as pltpu
from jax.sharding import PartitionSpec as P

F32 = jnp.float32
BF16 = jnp.bfloat16
MESH = pl.DeviceIdType.MESH
COPIES = 256


def split(value):
    high = value.astype(BF16)
    return high, (value - high.astype(F32)).astype(BF16)


def dot(left, right):
    return jnp.dot(left, right, preferred_element_type=F32)


def product(left, right):
    left_high, left_low = left
    right_high, right_low = right
    return dot(left_high, right_high) + (dot(left_high, right_low) + dot(left_low, right_high))


def product_t(left, right):
    def one(a, b):
        return lax.dot_general(a, b, (((0,), (0,)), ((), ())), preferred_element_type=F32)

    left_high, left_low = left
    right_high, right_low = right
    return one(left_high, right_high) + (one(left_high, right_low) + one(left_low, right_high))


def kernel(
    rhs_sub, rhs_anc, inv_sub, panel_mid, panel_anc, mask, inv_anc,
    x_sub, x_anc,
    rhs0, rhs1, inv0, inv1, mid, panels, anc, anc_rhs,
    first, tee, op_high, op_low, first_high, first_low,
    q_high, q_low, g_high, g_low,
    update, y_in, value, x_out, own,
    w_part, w_send, r_first, r_sum, r_second, out_sub, mask_tile,
    send_sem, recv_sem, local_sem,
):
    y = lax.axis_index("leaf")
    r = lax.axis_index("row")
    x, z, c = r // 8, (r // 2) % 4, r % 2
    o = 1 - c

    def at_x(d):
        return (y, ((x + d) % 4) * 8 + z * 2 + c)

    def at_z(d):
        return (y, x * 8 + ((z + d) % 4) * 2 + c)

    def at_y(d):
        return ((y + d) % 4, r)

    sibling = (y, x * 8 + z * 2 + o)
    ring = (1, 3, 2)

    count = [0, 0]
    sends = []

    def remote(src, dst, landing, device):
        index = count[0]
        count[0] += 1
        out = pltpu.make_async_remote_copy(
            src_ref=src, dst_ref=dst, send_sem=send_sem.at[index], recv_sem=recv_sem.at[index],
            device_id=device, device_id_type=MESH,
        )
        out.start()
        sends.append(out)
        into = pltpu.make_async_remote_copy(
            src_ref=landing, dst_ref=landing, send_sem=send_sem.at[index], recv_sem=recv_sem.at[index],
            device_id=device, device_id_type=MESH,
        )
        return into.wait_recv

    def local(src, dst):
        index = count[1]
        count[1] += 1
        copy = pltpu.make_async_copy(src, dst, local_sem.at[index])
        copy.start()
        return copy.wait

    def wait_all(waits):
        for wait in waits:
            wait()

    def columns(core, half):
        return pl.ds(pl.multiple_of(core * 256 + half * 128, 128), 128)

    def block(i):
        return pl.ds(pl.multiple_of(i * 256, 256), 256)

    mine = pl.ds(pl.multiple_of(c * 32, 32), 32)
    theirs = pl.ds(pl.multiple_of(o * 32, 32), 32)
    both = block(c)
    other = block(o)

    load_rhs0 = [local(rhs_sub.at[0, 0, :, columns(c, h)], rhs0.at[h, x, z, mine]) for h in range(2)]
    load_inv0 = [local(inv_sub.at[0, 0, pl.ds(16 * h, 16)], inv0.at[x, z, c, h]) for h in range(2)]
    load_rhs1 = [local(rhs_sub.at[0, 1, :, columns(c, h)], rhs1.at[h, mine]) for h in range(2)]
    load_inv1 = [local(inv_sub.at[0, 1, pl.ds(16 * h, 16)], inv1.at[x, z, c, h]) for h in range(2)]
    load_mid = [local(panel_mid.at[0, pl.ds(16 * h, 16)], mid.at[x, z, c, h]) for h in range(2)]
    for s in range(2):
        for j in range(4):
            mask_tile[c, s, j] = jnp.full((8, 128), mask[0, s, j].astype(F32), F32)

    barrier = pltpu.get_barrier_semaphore()
    for device in [at_x(1), at_x(2), at_x(3), at_z(1), at_z(2), at_z(3), at_y(1), at_y(2), at_y(3), sibling]:
        pl.semaphore_signal(barrier, inc=1, device_id=device, device_id_type=MESH)
    pl.semaphore_wait(barrier, 10)

    swap_rhs0 = [
        remote(rhs_sub.at[0, 0, :, columns(o, h)], rhs0.at[h, x, z, mine], rhs0.at[h, x, z, theirs], sibling)
        for h in range(2)
    ]

    def vector_start(ref):
        near, far = [[], []], [[], []]
        for d in ring:
            near[0].append(remote(ref.at[0, x, z], ref.at[0, x, z], ref.at[0, x, (z - d) % 4], at_z(d)))
            near[1].append(remote(ref.at[1, x, z], ref.at[1, x, z], ref.at[1, (x - d) % 4, z], at_x(d)))
        for d in ring:
            far[0].append(remote(ref.at[0, x, z], ref.at[0, x, z], ref.at[0, (x - d) % 4, z], at_x(d)))
            far[1].append(remote(ref.at[1, x, z], ref.at[1, x, z], ref.at[1, x, (z - d) % 4], at_z(d)))
        return near, far

    def vector_pass(ref, waits):
        near, far = waits
        for n, e in enumerate(ring):
            k = (z - e) % 4
            near[0][n]()
            for d in ring:
                far[0].append(remote(ref.at[0, x, k], ref.at[0, x, k], ref.at[0, (x - d) % 4, k], at_x(d)))
            k = (x - e) % 4
            near[1][n]()
            for d in ring:
                far[1].append(remote(ref.at[1, k, z], ref.at[1, k, z], ref.at[1, k, (z - d) % 4], at_z(d)))
        return far

    def vector_end(ref, far, high_ref, low_ref):
        for h in range(2):
            wait_all(far[h])
            high, low = split(ref[h].reshape(1024, 128))
            high_ref[:, 128 * h:128 * h + 128] = high
            low_ref[:, 128 * h:128 * h + 128] = low

    def matrix_share(ref):
        return [remote(ref.at[x, z, c], ref.at[x, z, c], ref.at[x, z, o], sibling)]

    def matrix_start(ref):
        near = [[], []]
        for d in ring:
            near[0].append(remote(ref.at[x, z, c, 0], ref.at[x, z, c, 0], ref.at[x, (z - d) % 4, c, 0], at_z(d)))
            near[1].append(remote(ref.at[x, z, c, 1], ref.at[x, z, c, 1], ref.at[(x - d) % 4, z, c, 1], at_x(d)))
        return near

    def matrix_near(ref, near):
        shared = []
        for n, d in enumerate(ring):
            near[0][n]()
            near[1][n]()
            k = (z - d) % 4
            shared.append(remote(ref.at[x, k, c, 0], ref.at[x, k, c, 0], ref.at[x, k, o, 0], sibling))
            k = (x - d) % 4
            shared.append(remote(ref.at[k, z, c, 1], ref.at[k, z, c, 1], ref.at[k, z, o, 1], sibling))
        return shared

    def matrix_far(ref, distances):
        far = []
        for d in distances:
            k = (x - d) % 4
            far.append((d, 0, remote(ref.at[x, :, c, 0], ref.at[x, :, c, 0], ref.at[k, :, c, 0], at_x(d))))
            k = (z - d) % 4
            far.append((d, 1, remote(ref.at[:, z, c, 1], ref.at[:, z, c, 1], ref.at[:, k, c, 1], at_z(d))))
        return far

    def matrix_end(ref, far):
        shared = []
        for d, h, wait in far:
            wait()
            if h == 0:
                k = (x - d) % 4
                shared.append(remote(ref.at[k, :, c, 0], ref.at[k, :, c, 0], ref.at[k, :, o, 0], sibling))
            else:
                k = (z - d) % 4
                shared.append(remote(ref.at[:, k, c, 1], ref.at[:, k, c, 1], ref.at[:, k, o, 1], sibling))
        return shared

    def masked(s):
        for core in range(2):
            for j in range(4):
                scale = mask_tile[core, s, j][0:1, 0:1]
                panels[s, core, 128 * j:128 * j + 128] = panels[s, core, 128 * j:128 * j + 128] * scale

    def panel(s):
        return panels[s].reshape(1024, 1024)

    def whole(ref):
        return ref[...].reshape(1024, 1024)

    def chip_rows(ref):
        return split(ref[x, z].reshape(64, 1024))

    wait_all(load_rhs0)
    wait_all(swap_rhs0)
    gather0 = vector_start(rhs0)
    wait_all(load_inv0)
    share_inv0 = matrix_share(inv0)
    swap_rhs1 = [
        remote(rhs_sub.at[0, 1, :, columns(o, h)], rhs1.at[h, mine], rhs1.at[h, theirs], sibling)
        for h in range(2)
    ]
    swap_mask = [remote(mask_tile.at[c], mask_tile.at[c], mask_tile.at[o], sibling)]
    wait_all(load_mid)
    share_mid = matrix_share(mid)
    wait_all(load_inv1)
    share_inv1 = matrix_share(inv1)
    gather0 = vector_pass(rhs0, gather0)
    near_inv1 = matrix_start(inv1)
    load_panels = [local(panel_anc.at[0, s], panels.at[s, c]) for s in (1, 0)]
    swap_panels = [remote(panel_anc.at[0, s], panels.at[s, c], panels.at[s, o], sibling) for s in (1, 0)]
    load_anc = [local(rhs_anc.at[:, both], anc_rhs.at[c]), local(inv_anc, anc.at[c])]
    swap_anc = [
        remote(rhs_anc.at[:, other], anc_rhs.at[c], anc_rhs.at[o], sibling),
        remote(inv_anc, anc.at[c], anc.at[o], sibling),
    ]
    wait_all(share_inv0)
    vector_end(rhs0, gather0, op_high, op_low)
    got = product(chip_rows(inv0), (op_high[...], op_low[...]))
    own[0] = got
    for h in range(2):
        first[h, x, z] = got[:, 128 * h:128 * h + 128]
    gather1 = vector_start(first)
    share_inv1 += matrix_near(inv1, near_inv1)
    gather1 = vector_pass(first, gather1)
    far_inv1 = matrix_far(inv1, (1, 3))
    wait_all(swap_mask)
    wait_all(load_panels)
    wait_all(swap_panels)
    masked(1)
    masked(0)
    wait_all(load_rhs1)
    wait_all(swap_rhs1)
    wait_all(share_mid)
    vector_end(first, gather1, first_high, first_low)
    got = product(chip_rows(mid), (first_high[...], first_low[...]))
    for h in range(2):
        tee[h, x, z] = rhs1[h] - got[:, 128 * h:128 * h + 128]
    gather2 = vector_start(tee)
    far_inv1 += matrix_far(inv1, (2,))
    gather2 = vector_pass(tee, gather2)
    update[...] = product(split(panel(0)), (first_high[...], first_low[...])).reshape(4, 256, 256)
    share_inv1 += matrix_end(inv1, far_inv1)
    wait_all(share_inv1)
    near_inv0 = matrix_start(inv0)
    near_mid = matrix_start(mid)
    for n in range(4):
        cols = slice(256 * n, 256 * n + 256)
        below = inv1[n:, :, :, :, :, cols].reshape(1024 - 256 * n, 256)
        left = panels[1, :, :, 256 * n:].reshape(1024, 1024 - 256 * n)
        high, low = split(product(split(left), split(below)))
        q_high[:, cols] = high
        q_low[:, cols] = low
    vector_end(tee, gather2, op_high, op_low)

    def update_block(i):
        rows = block(i)
        update[i] = update[i] + product((q_high[rows], q_low[rows]), (op_high[...], op_low[...]))

    update_in = []
    for d in ring:
        k = (y + d) % 4
        update_block(k)
        update_in.append(remote(update.at[k], y_in.at[d - 1], y_in.at[d - 1], at_y(d)))
    update_block(y)
    share_inv0 = matrix_near(inv0, near_inv0)
    far_inv0 = matrix_far(inv0, ring)
    share_mid = matrix_near(mid, near_mid)
    far_mid = matrix_far(mid, ring)
    own[1] = product(chip_rows(inv1), (op_high[...], op_low[...]))
    for s, ref in enumerate((inv0, inv1)):
        w_part[s] = product_t(chip_rows(ref), split(own[s]))
    wait_all(load_anc)
    wait_all(swap_anc)
    for n in range(4):
        cols = slice(256 * n, 256 * n + 256)
        high, low = split(product_t(split(whole(anc)), split(anc[:, :, cols].reshape(1024, 256))))
        g_high[:, cols] = high
        g_low[:, cols] = low
    wait_all(update_in)
    rows = block(y % 2)
    value[y] = anc_rhs[y // 2, rows] - ((update[y] + y_in[0]) + (y_in[1] + y_in[2]))
    value_in = [remote(value.at[y], value.at[y], value.at[(y - d) % 4], at_y(d)) for d in ring]
    share_inv0 += matrix_end(inv0, far_inv0)

    def solve_part(i):
        cols = block(i)
        return product((g_high[:, cols], g_low[:, cols]), split(value[i])).reshape(2, 512, 256)

    x_out[...] = solve_part(y)
    share_mid += matrix_end(mid, far_mid)
    for n, d in enumerate(ring):
        value_in[n]()
        x_out[...] += solve_part((y - d) % 4)
    high, low = split(x_out[...].reshape(1024, 256))
    op_high[...] = high
    op_low[...] = low

    def reduce_start(s):
        landed = {}
        for e in (2, 1, 3, 0):
            k = (z + e) % 4
            landed[0, e] = [
                remote(w_send.at[s, 0, (x + d) % 4, k], r_first.at[s, 0, d - 1, k], r_first.at[s, 0, d - 1, k], at_x(d))
                for d in ring
            ]
            k = (x + e) % 4
            landed[1, e] = [
                remote(w_send.at[s, 1, k, (z + d) % 4], r_first.at[s, 1, d - 1, k], r_first.at[s, 1, d - 1, k], at_z(d))
                for d in ring
            ]
        return landed

    def reduce_sum(s, landed, h, e):
        wait_all(landed[h, e])
        k = ((z if h == 0 else x) + e) % 4
        kept = w_send[s, 0, x, k] if h == 0 else w_send[s, 1, k, z]
        return (kept + r_first[s, h, 0, k]) + (r_first[s, h, 1, k] + r_first[s, h, 2, k])

    def reduce_pass(s, landed):
        waits = [[], []]
        for e in (2, 1, 3):
            for h in range(2):
                r_sum[s, h, e - 1] = reduce_sum(s, landed, h, e)
                device = at_z(e) if h == 0 else at_x(e)
                waits[h].append(
                    remote(r_sum.at[s, h, e - 1], r_second.at[s, h, e - 1], r_second.at[s, h, e - 1], device)
                )
        return waits

    def reduce_end(s, landed, waits):
        for h in range(2):
            total = reduce_sum(s, landed, h, 0)
            wait_all(waits[h])
            total += r_second[s, h, 0] + (r_second[s, h, 1] + r_second[s, h, 2])
            out_sub[s, :, 128 * h:128 * h + 128] = total
        out = remote(out_sub.at[s, theirs], x_sub.at[0, s, :, both], x_sub.at[0, s, :, other], sibling)
        return [out, local(out_sub.at[s, mine], x_sub.at[0, s, :, both])]

    def put(s, total):
        for h in range(2):
            w_send[s, h] = total[:, 128 * h:128 * h + 128].reshape(4, 4, 64, 128)

    total = w_part[1] - product_t((q_high[...], q_low[...]), (op_high[...], op_low[...]))
    put(1, total)
    landed1 = reduce_start(1)
    high, low = split(total)
    first_high[...] = high
    first_low[...] = low
    done = [remote(x_out.at[o], x_anc.at[:, both], x_anc.at[:, other], sibling)]
    done.append(local(x_out.at[c], x_anc.at[:, both]))
    total = product_t(split(panel(0)), (op_high[...], op_low[...]))
    wait_all(share_mid)
    total += product_t(split(whole(mid)), (first_high[...], first_low[...]))
    high, low = split(total)
    op_high[...] = high
    op_low[...] = low
    wait_all(share_inv0)
    put(0, w_part[0] - product_t(split(whole(inv0)), (op_high[...], op_low[...])))
    landed0 = reduce_start(0)
    waits1 = reduce_pass(1, landed1)
    done += reduce_end(1, landed1, waits1)
    waits0 = reduce_pass(0, landed0)
    done += reduce_end(0, landed0, waits0)
    wait_all(done)
    for copy in sends:
        copy.wait_send()


def per_device(rhs_sub, rhs_anc, inv_sub, panel_mid, panel_anc, block_mask, inv_anc):
    any_space = pl.BlockSpec(memory_space=pl.ANY)
    vmem = pltpu.VMEM
    return pl.pallas_call(
        kernel,
        out_shape=(
            jax.ShapeDtypeStruct((1, 2, 32, 512), F32),
            jax.ShapeDtypeStruct((512, 512), F32),
        ),
        in_specs=[any_space] * 5 + [pl.BlockSpec(memory_space=pltpu.SMEM), any_space],
        out_specs=(any_space, any_space),
        scratch_shapes=[
            vmem((2, 4, 4, 64, 128), F32),
            vmem((2, 64, 128), F32),
            vmem((4, 4, 2, 2, 16, 1024), F32),
            vmem((4, 4, 2, 2, 16, 1024), F32),
            vmem((4, 4, 2, 2, 16, 1024), F32),
            vmem((2, 2, 512, 1024), F32),
            vmem((2, 512, 1024), F32),
            vmem((2, 512, 256), F32),
            vmem((2, 4, 4, 64, 128), F32),
            vmem((2, 4, 4, 64, 128), F32),
            vmem((1024, 256), BF16),
            vmem((1024, 256), BF16),
            vmem((1024, 256), BF16),
            vmem((1024, 256), BF16),
            vmem((1024, 1024), BF16),
            vmem((1024, 1024), BF16),
            vmem((1024, 1024), BF16),
            vmem((1024, 1024), BF16),
            vmem((4, 256, 256), F32),
            vmem((3, 256, 256), F32),
            vmem((4, 256, 256), F32),
            vmem((2, 512, 256), F32),
            vmem((2, 64, 256), F32),
            vmem((2, 1024, 256), F32),
            vmem((2, 2, 4, 4, 64, 128), F32),
            vmem((2, 2, 3, 4, 64, 128), F32),
            vmem((2, 2, 3, 64, 128), F32),
            vmem((2, 2, 3, 64, 128), F32),
            vmem((2, 64, 256), F32),
            vmem((2, 2, 4, 8, 128), F32),
            pltpu.SemaphoreType.DMA((COPIES,)),
            pltpu.SemaphoreType.DMA((COPIES,)),
            pltpu.SemaphoreType.DMA((32,)),
        ],
        compiler_params=pltpu.CompilerParams(
            collective_id=0, has_side_effects=True, vmem_limit_bytes=60 * 2**20
        ),
        cost_estimate=pl.CostEstimate(flops=3 * 2 * 2900 * 2**20, bytes_accessed=10 * 2**20, transcendentals=0),
        name="solve",
    )(rhs_sub, rhs_anc, inv_sub, panel_mid, panel_anc, block_mask, inv_anc)


def solution(mesh):
    return jax.shard_map(
        per_device,
        mesh=mesh,
        in_specs=(
            P("leaf", None, "row", None),
            P("row", None),
            P("leaf", None, "row", None),
            P("leaf", "row", None),
            P("leaf", None, "row", None),
            P("leaf", None, "row"),
            P("row", None),
        ),
        out_specs=(P("leaf", None, "row", None), P("row", None)),
        check_vma=False,
    )
```

time: 636 us -> 123 us (0.19); the launches traced: 626 us -> 123 us
  waiting for transfers between devices: 530 us -> 0 us
  Pallas kernels: 0 us -> 118 us
  matrix products: 60 us -> 0 us
  between operations: 14.5 us -> 0.64 us
  local copies, waits for them, and re-layouts: 13.2 us -> 3.83 us
    all_gather x4 -> x0, waiting for transfers between devices: 170 us -> none  [the longest x2 92.9 us: solve_rows(): return product(matrix, lax.all_gather(rhs_local, 'row', axis=0, tiled=True))]
    reduce_scatter x2 -> x0, waiting for transfers between devices: 156 us -> none  [the longest x1 78.3 us: per_device(): lax.psum_scatter(ancestor_part + transposed(middle, x_second), 'row', sca...]
    unnamed x11 -> x0, waiting for transfers between devices: 155 us -> none
    pallas_call x0 -> x1, Pallas kernels: none -> 118 us  [per_device(): pl.pallas_call(kernel, out_shape=(jax.ShapeDtypeStruct((1, 2, 32, 512), F...]
    dot_general x12 -> x0, matrix products: 60 us -> none  [the longest x6 30.8 us: transposed(): lax.dot_general(left, right, (((0,), (0,)), ((), ())), precision=lax.Prec...]
    psum x1 -> x0, waiting for transfers between devices: 43.3 us -> none  [per_device(): total = lax.psum(partial_value, 'leaf')]
  transfers between devices with their start and end apart: 11 -> 0, of which waited for: 11 -> 0; matrix products, arithmetic and copies ran while one was open for 2% -> 0% of each run, Pallas kernels for 0% -> 0%
where the time goes in v2:
time: 123 us
  Pallas kernels  118 us (96%)
  local copies, waits for them, and re-layouts  3.83 us (3%)
    pallas_call x1, Pallas kernels, per_device(): pl.pallas_call(kernel, out_shape=(jax.ShapeDtypeStruct((1, 2, 32, 512), F...  118 us
    unnamed x2, local copies, waits for them, and re-layouts  3.83 us

profile of v2, /device:TPU:1, one launch (start us, length us, event | category | flops | bytes accessed | tf_op | source)
XLA Modules:
  0.0 122.6 jit_solution(18272815064961739764)
XLA Ops:
  0.6 118.2 %solve.1 = (f32[1,2,32,512]{3,2,1,0:T(8,128)}, f32[512,512]{1,0:T(8,128)}) custom-call(f32[1,2,32,512]{3,2,1,0:T(8,128)} %rhs_sub.1, f32[512,512]{1,0:T(8,128)} %rhs_anc.1, f32[1,2,32,1024]{3,2,1,0:T(8,128)} %inv_sub.1, f32[1,32,1024]{2,1,0:T(8,128)} %panel_mid.1, f32[1,2,512,1024]{3,2,1,0:T(8,128)} %panel_anc.1, s32[1,2,4]{2,1,0:T(2,128)} %mask.1, ...), custom_call_target="tpu_custom_call" | custom-call | flops 18245222400 | bytes 10485760 | tf_op jit(solution)/shard_map/solve/pallas_call | solution.py:392
  118.8 1.6 %copy.11 = f32[1,2,32,512]{3,2,1,0:T(8,128)} copy(f32[1,2,32,512]{3,2,1,0:T(8,128)} %get-tuple-element.4) | data formatting | bytes 262144
  120.4 2.3 %copy.12 = f32[512,512]{1,0:T(8,128)} copy(f32[512,512]{1,0:T(8,128)} %get-tuple-element.5) | data formatting | bytes 2097152

commit v3 on v2

--- a/solution.py
+++ b/solution.py
@@ -226,13 +226,12 @@
     share_inv1 = matrix_share(inv1)
     gather0 = vector_pass(rhs0, gather0)
     near_inv1 = matrix_start(inv1)
-    load_panels = [local(panel_anc.at[0, s], panels.at[s, c]) for s in (1, 0)]
-    swap_panels = [remote(panel_anc.at[0, s], panels.at[s, c], panels.at[s, o], sibling) for s in (1, 0)]
-    load_anc = [local(rhs_anc.at[:, both], anc_rhs.at[c]), local(inv_anc, anc.at[c])]
-    swap_anc = [
-        remote(rhs_anc.at[:, other], anc_rhs.at[c], anc_rhs.at[o], sibling),
-        remote(inv_anc, anc.at[c], anc.at[o], sibling),
-    ]
+    load_anc = [local(inv_anc, anc.at[c])]
+    swap_anc = [remote(inv_anc, anc.at[c], anc.at[o], sibling)]
+    load_panels = [local(panel_anc.at[0, s], panels.at[s, c]) for s in range(2)]
+    swap_panels = [remote(panel_anc.at[0, s], panels.at[s, c], panels.at[s, o], sibling) for s in range(2)]
+    load_anc_rhs = [local(rhs_anc.at[:, both], anc_rhs.at[c])]
+    swap_anc_rhs = [remote(rhs_anc.at[:, other], anc_rhs.at[c], anc_rhs.at[o], sibling)]
     wait_all(share_inv0)
     vector_end(rhs0, gather0, op_high, op_low)
     got = product(chip_rows(inv0), (op_high[...], op_low[...]))
@@ -243,11 +242,13 @@
     share_inv1 += matrix_near(inv1, near_inv1)
     gather1 = vector_pass(first, gather1)
     far_inv1 = matrix_far(inv1, (1, 3))
-    wait_all(swap_mask)
-    wait_all(load_panels)
-    wait_all(swap_panels)
-    masked(1)
-    masked(0)
+    wait_all(load_anc)
+    wait_all(swap_anc)
+    for n in range(4):
+        cols = slice(256 * n, 256 * n + 256)
+        high, low = split(product_t(split(whole(anc)), split(anc[:, :, cols].reshape(1024, 256))))
+        g_high[:, cols] = high
+        g_low[:, cols] = low
     wait_all(load_rhs1)
     wait_all(swap_rhs1)
     wait_all(share_mid)
@@ -258,10 +259,15 @@
     gather2 = vector_start(tee)
     far_inv1 += matrix_far(inv1, (2,))
     gather2 = vector_pass(tee, gather2)
+    near_inv0 = matrix_start(inv0)
+    wait_all(swap_mask)
+    wait_all(load_panels)
+    wait_all(swap_panels)
+    masked(0)
     update[...] = product(split(panel(0)), (first_high[...], first_low[...])).reshape(4, 256, 256)
+    masked(1)
     share_inv1 += matrix_end(inv1, far_inv1)
     wait_all(share_inv1)
-    near_inv0 = matrix_start(inv0)
     near_mid = matrix_start(mid)
     for n in range(4):
         cols = slice(256 * n, 256 * n + 256)
@@ -270,6 +276,8 @@
         high, low = split(product(split(left), split(below)))
         q_high[:, cols] = high
         q_low[:, cols] = low
+    share_inv0 = matrix_near(inv0, near_inv0)
+    far_inv0 = matrix_far(inv0, ring)
     vector_end(tee, gather2, op_high, op_low)
 
     def update_block(i):
@@ -282,20 +290,13 @@
         update_block(k)
         update_in.append(remote(update.at[k], y_in.at[d - 1], y_in.at[d - 1], at_y(d)))
     update_block(y)
-    share_inv0 = matrix_near(inv0, near_inv0)
-    far_inv0 = matrix_far(inv0, ring)
     share_mid = matrix_near(mid, near_mid)
     far_mid = matrix_far(mid, ring)
     own[1] = product(chip_rows(inv1), (op_high[...], op_low[...]))
     for s, ref in enumerate((inv0, inv1)):
         w_part[s] = product_t(chip_rows(ref), split(own[s]))
-    wait_all(load_anc)
-    wait_all(swap_anc)
-    for n in range(4):
-        cols = slice(256 * n, 256 * n + 256)
-        high, low = split(product_t(split(whole(anc)), split(anc[:, :, cols].reshape(1024, 256))))
-        g_high[:, cols] = high
-        g_low[:, cols] = low
+    wait_all(load_anc_rhs)
+    wait_all(swap_anc_rhs)
     wait_all(update_in)
     rows = block(y % 2)
     value[y] = anc_rhs[y // 2, rows] - ((update[y] + y_in[0]) + (y_in[1] + y_in[2]))
@@ -307,7 +308,6 @@
         return product((g_high[:, cols], g_low[:, cols]), split(value[i])).reshape(2, 512, 256)
 
     x_out[...] = solve_part(y)
-    share_mid += matrix_end(mid, far_mid)
     for n, d in enumerate(ring):
         value_in[n]()
         x_out[...] += solve_part((y - d) % 4)
@@ -363,6 +363,7 @@
     total = w_part[1] - product_t((q_high[...], q_low[...]), (op_high[...], op_low[...]))
     put(1, total)
     landed1 = reduce_start(1)
+    share_mid += matrix_end(mid, far_mid)
     high, low = split(total)
     first_high[...] = high
     first_low[...] = low

time: 123 us -> 125 us (1.016)
  Pallas kernels: 118 us -> 120 us
    pallas_call x1, Pallas kernels: 118 us -> 120 us  [per_device(): pl.pallas_call(kernel, out_shape=(jax.ShapeDtypeStruct((1, 2, 32, 512), F...]
where the time goes in v3:
time: 125 us
  Pallas kernels  120 us (96%)
  local copies, waits for them, and re-layouts  3.83 us (3%)
    pallas_call x1, Pallas kernels, per_device(): pl.pallas_call(kernel, out_shape=(jax.ShapeDtypeStruct((1, 2, 32, 512), F...  120 us
    unnamed x2, local copies, waits for them, and re-layouts  3.83 us

profile of v3, /device:TPU:1, one launch (start us, length us, event | category | flops | bytes accessed | tf_op | source)
XLA Modules:
  0.0 124.9 jit_solution(3371250691111270413)
XLA Ops:
  0.6 120.4 %solve.1 = (f32[1,2,32,512]{3,2,1,0:T(8,128)}, f32[512,512]{1,0:T(8,128)}) custom-call(f32[1,2,32,512]{3,2,1,0:T(8,128)} %rhs_sub.1, f32[512,512]{1,0:T(8,128)} %rhs_anc.1, f32[1,2,32,1024]{3,2,1,0:T(8,128)} %inv_sub.1, f32[1,32,1024]{2,1,0:T(8,128)} %panel_mid.1, f32[1,2,512,1024]{3,2,1,0:T(8,128)} %panel_anc.1, s32[1,2,4]{2,1,0:T(2,128)} %mask.1, ...), custom_call_target="tpu_custom_call" | custom-call | flops 18245222400 | bytes 10485760 | tf_op jit(solution)/shard_map/solve/pallas_call | solution.py:393
  121.1 1.6 %copy.11 = f32[1,2,32,512]{3,2,1,0:T(8,128)} copy(f32[1,2,32,512]{3,2,1,0:T(8,128)} %get-tuple-element.4) | data formatting | bytes 262144
  122.6 2.3 %copy.12 = f32[512,512]{1,0:T(8,128)} copy(f32[512,512]{1,0:T(8,128)} %get-tuple-element.5) | data formatting | bytes 2097152

commit v4 on v3

--- a/solution.py
+++ b/solution.py
@@ -259,7 +259,6 @@
     gather2 = vector_start(tee)
     far_inv1 += matrix_far(inv1, (2,))
     gather2 = vector_pass(tee, gather2)
-    near_inv0 = matrix_start(inv0)
     wait_all(swap_mask)
     wait_all(load_panels)
     wait_all(swap_panels)
@@ -268,6 +267,7 @@
     masked(1)
     share_inv1 += matrix_end(inv1, far_inv1)
     wait_all(share_inv1)
+    near_inv0 = matrix_start(inv0)
     near_mid = matrix_start(mid)
     for n in range(4):
         cols = slice(256 * n, 256 * n + 256)
@@ -276,8 +276,6 @@
         high, low = split(product(split(left), split(below)))
         q_high[:, cols] = high
         q_low[:, cols] = low
-    share_inv0 = matrix_near(inv0, near_inv0)
-    far_inv0 = matrix_far(inv0, ring)
     vector_end(tee, gather2, op_high, op_low)
 
     def update_block(i):
@@ -290,6 +288,8 @@
         update_block(k)
         update_in.append(remote(update.at[k], y_in.at[d - 1], y_in.at[d - 1], at_y(d)))
     update_block(y)
+    share_inv0 = matrix_near(inv0, near_inv0)
+    far_inv0 = matrix_far(inv0, ring)
     share_mid = matrix_near(mid, near_mid)
     far_mid = matrix_far(mid, ring)
     own[1] = product(chip_rows(inv1), (op_high[...], op_low[...]))
@@ -308,6 +308,7 @@
         return product((g_high[:, cols], g_low[:, cols]), split(value[i])).reshape(2, 512, 256)
 
     x_out[...] = solve_part(y)
+    share_mid += matrix_end(mid, far_mid)
     for n, d in enumerate(ring):
         value_in[n]()
         x_out[...] += solve_part((y - d) % 4)
@@ -363,7 +364,6 @@
     total = w_part[1] - product_t((q_high[...], q_low[...]), (op_high[...], op_low[...]))
     put(1, total)
     landed1 = reduce_start(1)
-    share_mid += matrix_end(mid, far_mid)
     high, low = split(total)
     first_high[...] = high
     first_low[...] = low

time: 125 us -> 124 us (level)
  no operation moved by 1% of the time
where the time goes in v4:
time: 124 us
  Pallas kernels  119 us (96%)
  local copies, waits for them, and re-layouts  3.83 us (3%)
    pallas_call x1, Pallas kernels, per_device(): pl.pallas_call(kernel, out_shape=(jax.ShapeDtypeStruct((1, 2, 32, 512), F...  119 us
    unnamed x2, local copies, waits for them, and re-layouts  3.83 us

profile of v4, /device:TPU:1, one launch (start us, length us, event | category | flops | bytes accessed | tf_op | source)
XLA Modules:
  0.0 123.9 jit_solution(7207034002847114188)
XLA Ops:
  0.6 119.4 %solve.1 = (f32[1,2,32,512]{3,2,1,0:T(8,128)}, f32[512,512]{1,0:T(8,128)}) custom-call(f32[1,2,32,512]{3,2,1,0:T(8,128)} %rhs_sub.1, f32[512,512]{1,0:T(8,128)} %rhs_anc.1, f32[1,2,32,1024]{3,2,1,0:T(8,128)} %inv_sub.1, f32[1,32,1024]{2,1,0:T(8,128)} %panel_mid.1, f32[1,2,512,1024]{3,2,1,0:T(8,128)} %panel_anc.1, s32[1,2,4]{2,1,0:T(2,128)} %mask.1, ...), custom_call_target="tpu_custom_call" | custom-call | flops 18245222400 | bytes 10485760 | tf_op jit(solution)/shard_map/solve/pallas_call | solution.py:393
  120.0 1.6 %copy.11 = f32[1,2,32,512]{3,2,1,0:T(8,128)} copy(f32[1,2,32,512]{3,2,1,0:T(8,128)} %get-tuple-element.4) | data formatting | bytes 262144
  121.6 2.3 %copy.12 = f32[512,512]{1,0:T(8,128)} copy(f32[512,512]{1,0:T(8,128)} %get-tuple-element.5) | data formatting | bytes 2097152
